TPU v7x, 512 devices: a whole 4x4x16 slice. The times are simulated.
512 devices in a mesh: row: 32 (over x, y, core), col: 16 (over z).
Axes of the slice: x: 4, y: 4, z: 16, core: 2. Of those that a mesh axis runs over, the one named last changes fastest.
Arguments:
- delta: bfloat16 [29568, 8192], P('row', 'col'), may hold values from -0.03125 to 0.03125
- probe: bfloat16 [8192, 256], P('col'), may hold values from -6 to 6
Outputs:
- q_basis: float32 [29568, 256], P('row')
- w_basis: float32 [8192, 256], P('col')
- core: float32 [256, 256], replicated
All inputs are finite; a program needn't handle non-finite values.
Results may differ from a plain program's by a relative error of at most 0.0045.
Values may be sent and summed in bfloat16 or wider, within the bound.
A program may use at most 64 MiB of HBM per device.

v0:
```python
import math

import jax
import jax.numpy as jnp
from jax import lax
from jax.sharding import PartitionSpec as P

D = 8192
FF = 29568
POWER = 2


def factor(matrix, gram):
    lower = jnp.linalg.cholesky(gram)
    basis = jax.scipy.linalg.solve_triangular(lower, matrix.T, lower=True).T
    return (basis, lower.T)


def local_gram(matrix):
    return jnp.dot(
        matrix.T, matrix, precision=lax.Precision.HIGHEST, preferred_element_type=jnp.float32
    )


def local(delta, probe):
    row_count = delta.shape[0]

    def range_step(right, last):
        partial_sketch = jnp.dot(delta, right, preferred_element_type=jnp.float32)
        padding = -row_count % lax.axis_size("col")
        padded = jnp.pad(partial_sketch, ((0, padding), (0, 0)))
        share = lax.psum_scatter(padded, "col", scatter_dimension=0, tiled=True)
        gram = lax.psum(local_gram(share), ("row", "col"))
        piece, upper = factor(share, gram)
        if last:
            full = lax.all_gather(piece, "col", axis=0, tiled=True)
        else:
            full = lax.all_gather(piece.astype(jnp.bfloat16), "col", axis=0, tiled=True)
        return (full[:row_count], upper)

    basis, upper = range_step(probe, POWER == 0)
    right = None
    for step in range(POWER):
        rounded = basis
        back = lax.dot_general(
            delta, rounded, (((0,), (0,)), ((), ())), preferred_element_type=jnp.float32
        )
        total = lax.psum(back, "row")
        gram = lax.psum(local_gram(total), "col")
        right, _ = factor(total, gram)
        basis, upper = range_step(right.astype(jnp.bfloat16), step + 1 == POWER)
    return (math.sqrt(FF) * basis, math.sqrt(D) * right, upper)


def solution(mesh):
    in_specs = (P("row", "col"), P("col", None))
    out_specs = (P("row", None), P("col", None), P())
    return jax.shard_map(local, mesh=mesh, in_specs=in_specs, out_specs=out_specs, check_vma=False)
```

profile of v0, /device:TPU:1, one launch (start us, length us, event | category | flops | bytes accessed | tf_op | source)
XLA Modules:
  0.0 2483.6 jit_solution(10620434221328743955)
XLA Ops:
  9.8 36.7 %fusion = f32[64,256]{1,0:T(8,128)S(1)} fusion(f32[928,256]{1,0:T(8,128)S(1)} %pad.11), kind=kCustom, calls=%all-reduce-scatter | all-reduce-scatter fusion | flops 262145 | bytes 1017856
  46.5 2.3 collective-permute-start
  48.9 2.3 collective-permute-start.1
  54.8 463.9 %all-reduce.18.cloned.1.call-done = f32[256,256]{0,1:T(8,128)} async-done(((f32[256,256]{0,1:T(8,128)}), f32[256,256]{0,1:T(8,128)}) %all-reduce.18.cloned.1.call-update) | async-done | bytes 262160 | tf_op jit(solution)/shard_map/psum | solution.py:33
  519.9 11.7 cholesky.256
  531.6 9.8 custom-call.21
  542.0 11.7 cholesky.273
  555.9 4.4 while.10
  560.3 19.7 custom-call.22
  580.6 24.9 %all-gather = bf16[16,58,256]{2,1,0:T(8,128)(2,1)S(1)} all-gather(bf16[1,58,256]{2,1,0:T(8,128)(2,1)S(1)} %fusion.73), channel_id=1, replica_groups=mesh['row'=32,'col'=16] {'col'}, dimensions={0}, use_global_device_ids=true | all-gather | bytes 504832 | tf_op jit(solution)/shard_map/all_gather | solution.py:38
  607.0 135.7 %all-reduce.20.cloned.1.call-done = f32[512,256]{0,1:T(8,128)} async-done(((f32[512,256]{0,1:T(8,128)}), f32[512,256]{0,1:T(8,128)}) %all-reduce.20.cloned.1.call-update) | async-done | bytes 524304 | tf_op jit(solution)/shard_map/psum | solution.py:48
  742.7 2.5 fusion.88
  745.3 126.3 %all-reduce.22.cloned.1.call-done = f32[256,256]{0,1:T(8,128)} async-done(((f32[256,256]{0,1:T(8,128)}), f32[256,256]{0,1:T(8,128)}) %all-reduce.22.cloned.1.call-update) | async-done | bytes 262160 | tf_op jit(solution)/shard_map/psum | solution.py:49
  872.8 11.7 cholesky.290
  885.2 9.8 custom-call.23
  895.5 11.7 cholesky.307
  909.4 14.6 while.11
  920.6 1.4 bitcast_dynamic-update-slice_fusion.11
  922.6 1.4 bitcast_dynamic-update-slice_fusion.11
  924.1 19.7 custom-call.24
  945.5 29.4 %fusion.1 = f32[64,256]{1,0:T(8,128)S(1)} fusion(f32[928,256]{1,0:T(8,128)S(1)} %pad.12), kind=kCustom, calls=%all-reduce-scatter.1 | all-reduce-scatter fusion | flops 262145 | bytes 1017856
  974.9 2.5 collective-permute-start.2
  977.4 2.4 collective-permute-start.3
  982.4 473.4 %all-reduce.24.cloned.1.call-done = f32[256,256]{0,1:T(8,128)} async-done(((f32[256,256]{0,1:T(8,128)}), f32[256,256]{0,1:T(8,128)}) %all-reduce.24.cloned.1.call-update) | async-done | bytes 262160 | tf_op jit(solution)/shard_map/psum | solution.py:33
  1457.0 11.7 cholesky.324
  1469.4 9.8 custom-call.25
  1479.7 11.7 cholesky.341
  1493.6 4.5 while.12
  1498.1 19.7 custom-call.26
  1518.4 24.9 %all-gather.1 = bf16[16,58,256]{2,1,0:T(8,128)(2,1)S(1)} all-gather(bf16[1,58,256]{2,1,0:T(8,128)(2,1)S(1)} %fusion.72), channel_id=1, replica_groups=mesh['row'=32,'col'=16] {'col'}, dimensions={0}, use_global_device_ids=true | all-gather | bytes 504832 | tf_op jit(solution)/shard_map/all_gather | solution.py:38
  1544.8 135.8 %all-reduce.26.cloned.1.call-done = f32[512,256]{0,1:T(8,128)} async-done(((f32[512,256]{0,1:T(8,128)}), f32[512,256]{0,1:T(8,128)}) %all-reduce.26.cloned.1.call-update) | async-done | bytes 524304 | tf_op jit(solution)/shard_map/psum | solution.py:48
  1680.6 2.5 fusion.89
  1683.2 126.2 %all-reduce.28.cloned.1.call-done = f32[256,256]{0,1:T(8,128)} async-done(((f32[256,256]{0,1:T(8,128)}), f32[256,256]{0,1:T(8,128)}) %all-reduce.28.cloned.1.call-update) | async-done | bytes 262160 | tf_op jit(solution)/shard_map/psum | solution.py:49
  1810.6 11.7 cholesky.358
  1823.0 9.8 custom-call.27
  1833.3 11.7 cholesky.375
  1847.2 4.3 while.13
  1851.5 19.7 custom-call.28
  1872.9 29.4 %fusion.2 = f32[64,256]{1,0:T(8,128)S(1)} fusion(f32[928,256]{1,0:T(8,128)S(1)} %pad.13), kind=kCustom, calls=%all-reduce-scatter.2 | all-reduce-scatter fusion | flops 262145 | bytes 1017856
  1902.3 2.2 collective-permute-start.4
  1904.5 2.7 collective-permute-start.5
  1910.8 472.1 %all-reduce.30.cloned.1.call-done = f32[256,256]{0,1:T(8,128)} async-done(((f32[256,256]{0,1:T(8,128)}), f32[256,256]{0,1:T(8,128)}) %all-reduce.30.cloned.1.call-update) | async-done | bytes 262160 | tf_op jit(solution)/shard_map/psum | solution.py:33
  2384.1 11.7 cholesky.392
  2396.5 9.8 custom-call.29
  2406.8 11.7 cholesky.409
  2421.5 4.1 while.14
  2425.6 19.9 custom-call.30
  2446.1 29.2 %all-gather.2 = f32[16,58,256]{2,1,0:T(8,128)S(1)} all-gather(f32[1,58,256]{2,1,0:T(8,128)S(1)} %maximum_bitcast_fusion), channel_id=1, replica_groups=mesh['row'=32,'col'=16] {'col'}, dimensions={0}, use_global_device_ids=true | all-gather | bytes 1009664 | tf_op jit(solution)/shard_map/all_gather | solution.py:36
  (171 shorter events, 54.6 us)
Async XLA Ops:
  7.2 1.2 copy-start
  7.2 511.5 %all-reduce.18.cloned.1.call-start = ((), (), s32[]{:S(2)}) async-start(), calls=%async_computation | async-start | bytes 524288 | tf_op jit(solution)/shard_map/psum | solution.py:33
  46.5 6.7 collective-permute-start
  48.9 4.3 collective-permute-start.1
  54.7 688.0 %all-reduce.20.cloned.1.call-start = ((), (), s32[]{:S(2)}) async-start(), calls=%async_computation.1 | async-start | bytes 1048576 | tf_op jit(solution)/shard_map/psum | solution.py:48
  518.7 1.2 copy-start.3
  607.0 264.6 %all-reduce.22.cloned.1.call-start = ((), (), s32[]{:S(2)}) async-start(), calls=%async_computation.2 | async-start | bytes 524288 | tf_op jit(solution)/shard_map/psum | solution.py:49
  745.3 710.5 %all-reduce.24.cloned.1.call-start = ((), (), s32[]{:S(2)}) async-start(), calls=%async_computation.3 | async-start | bytes 524288 | tf_op jit(solution)/shard_map/psum | solution.py:33
  871.6 1.2 copy-start.6
  909.3 34.4 %copy-start.1 = (f32[512,256]{0,1:T(8,128)S(1)}, f32[512,256]{0,1:T(8,128)}, u32[]{:S(2)}) copy-start(f32[512,256]{0,1:T(8,128)} %all-reduce.20.cloned.1.call-done) | copy-start | bytes 1572868
  974.9 5.9 collective-permute-start.2
  977.4 3.4 collective-permute-start.3
  982.3 698.3 %all-reduce.26.cloned.1.call-start = ((), (), s32[]{:S(2)}) async-start(), calls=%async_computation.4 | async-start | bytes 1048576 | tf_op jit(solution)/shard_map/psum | solution.py:48
  1455.8 1.2 copy-start.5
  1544.8 264.6 %all-reduce.28.cloned.1.call-start = ((), (), s32[]{:S(2)}) async-start(), calls=%async_computation.5 | async-start | bytes 524288 | tf_op jit(solution)/shard_map/psum | solution.py:49
  1683.1 699.7 %all-reduce.30.cloned.1.call-start = ((), (), s32[]{:S(2)}) async-start(), calls=%async_computation.6 | async-start | bytes 524288 | tf_op jit(solution)/shard_map/psum | solution.py:33
  1809.4 1.2 copy-start.7
  1847.1 24.0 copy-start.2
  1902.3 5.9 collective-permute-start.4
  1904.5 3.7 collective-permute-start.5
  2382.9 1.2 copy-start.4
Sparse Core Ops, SparseCore 0:
  54.8 463.7 all-reduce.17
  607.1 135.6 all-reduce.19
  745.6 125.9 all-reduce.21
  982.4 473.2 all-reduce.23
  1544.9 135.6 all-reduce.25
  1683.4 125.8 all-reduce.27
  1909.9 472.9 all-reduce.29
where the time goes:
time: 2490 us; the launch traced here: 2480 us
  waiting for transfers between devices  1940 us (78%)
  other arithmetic  273 us (11%)
  blocking collectives  175 us (7%)
  local copies, waits for them, and re-layouts  32.3 us (1%)
    psum x3, waiting for transfers between devices, range_step(): gram = lax.psum(local_gram(share), ('row', 'col'))  1410 us
    psum x2, waiting for transfers between devices, local(): total = lax.psum(back, 'row')  272 us
    psum x2, waiting for transfers between devices, local(): gram = lax.psum(local_gram(total), 'col')  252 us
    another operation x34, other arithmetic, factor(): lower = jnp.linalg.cholesky(gram)  173 us
    another operation x10, other arithmetic, factor(): basis = jax.scipy.linalg.solve_triangular(lower, matrix.T, lower=True).T  98.7 us
    unnamed x3, blocking collectives  95.4 us
    all_gather x2, blocking collectives, range_step(): full = lax.all_gather(piece.astype(jnp.bfloat16), 'col', axis=0, tiled=True)  49.9 us
  transfers between devices with their start and end apart: 13, of which 9 were waited for; matrix products, arithmetic and copies ran while one was open for 0% of the time, Pallas kernels for 0%

commit v1 on v0

v1 whole, which is shorter than its diff:
```python
import math

import jax
import jax.numpy as jnp
from jax import lax
from jax.experimental import pallas as pl
from jax.experimental.pallas import tpu as pltpu
from jax.sharding import PartitionSpec as P

D = 8192
FF = 29568
R = 256
POWER = 2

F32 = jnp.float32
BF16 = jnp.bfloat16
HIGHEST = lax.Precision.HIGHEST
MESH = pl.DeviceIdType.MESH

NZ = 16
NC = 16
CH = 64
ROWS = NZ * CH
COLS = D // NZ
PANEL = 64


def dot(a, b, dims):
    return lax.dot_general(a, b, (dims, ((), ())), precision=HIGHEST, preferred_element_type=F32)


def dot16(a, b):
    return jnp.dot(a, b, preferred_element_type=F32)


def split(x):
    high = x.astype(BF16)
    rest = x - high.astype(F32)
    middle = rest.astype(BF16)
    low = (rest - middle.astype(F32)).astype(BF16)
    return high, middle, low


def eliminate(block):
    groups = PANEL // 8
    t = [block[8 * g : 8 * g + 8, :] for g in range(groups)]
    sub = lax.broadcasted_iota(jnp.int32, (8, 128), 0)
    for q in range(groups):
        left = groups - q
        cols = [
            [jnp.broadcast_to(t[g][:, 8 * q + j : 8 * q + j + 1], (8, 128)) for j in range(8)]
            for g in range(q, groups)
        ]
        rows = [jnp.broadcast_to(t[q][j : j + 1, :], (8, 128)) for j in range(8)]
        lower = [[None] * 8 for _ in range(left)]
        for j in range(8):
            own = [jnp.broadcast_to(cols[0][j][m : m + 1, :], (8, 128)) for m in range(j, 8)]
            inverse = 1.0 / own[0]
            root = lax.rsqrt(own[0])
            for m in range(j + 1, 8):
                ratio = own[m - j] * inverse
                for g in range(left):
                    cols[g][m] = cols[g][m] - cols[g][j] * ratio
                rows[m] = rows[m] - rows[j] * ratio
            rows[j] = rows[j] * root
            for g in range(1, left):
                lower[g][j] = cols[g][j] * root
        for g in range(1, left):
            total = lower[g][0] * rows[0]
            for j in range(1, 8):
                total = total + lower[g][j] * rows[j]
            t[q + g] = t[q + g] - total
        done = rows[0]
        for j in range(1, 8):
            done = jnp.where(sub == j, rows[j], done)
        t[q] = done
    return jnp.concatenate(t, 0)


def factor_start(work, gram):
    at = lax.broadcasted_iota(jnp.int32, (R, R), 0)
    to = lax.broadcasted_iota(jnp.int32, (R, R), 1)
    work[:, :R] = gram[...]
    work[:, R:] = jnp.where(at == to, 1.0, 0.0).astype(F32)


def factor_panel(work, k):
    lane = lax.broadcasted_iota(jnp.int32, (PANEL, 128), 1)
    row = lax.broadcasted_iota(jnp.int32, (PANEL, 128), 0)
    wide = lax.broadcasted_iota(jnp.int32, (PANEL, R), 1)
    first = pl.multiple_of(k * PANEL, PANEL)
    panel = work[pl.ds(first, PANEL), :]
    block = pltpu.roll(panel[:, :R], R - k * PANEL, 1)[:, :128]
    block = jnp.where(lane < PANEL, block, jnp.where(lane == row + PANEL, 1.0, 0.0))
    inverse = eliminate(block)[:, PANEL : 2 * PANEL]
    upper = dot(inverse, panel, ((1,), (0,)))
    work[pl.ds(first, PANEL), :] = upper
    below = jnp.where(wide >= (k + 1) * PANEL, upper[:, :R], 0.0)
    work[...] = work[...] - dot(below, upper, ((0,), (0,)))


def lower_inverse(work):
    at = lax.broadcasted_iota(jnp.int32, (R, R), 0)
    to = lax.broadcasted_iota(jnp.int32, (R, R), 1)
    return jnp.where(at >= to, work[:, R:], 0.0)


def kernel(
    delta, delta_t, probe, q_out, w_out, core_out,
    part, full, arrived, basis, back, back_part, feature, gram, gram_part, gram_v, work, inv, xs, gz, piece,
    g_half, g_in, g_own, p_half, p_in, p_own,
    rs_send, rs_recv, ag_send, ag_recv, gz_send, gz_recv,
    c_send, c_recv, gs_send, gs_recv, ga_send, ga_recv, ps_send, ps_recv, pa_send, pa_recv,
    va_send, va_recv,
):
    r = lax.axis_index("row")
    z = lax.axis_index("col")
    chip = r // 2
    core = r % 2

    def along(step):
        return (r, lax.rem(z + step + NZ, NZ))

    def chip_at(step):
        return lax.rem(chip + step, NC)

    def device(other):
        return (2 * other + core, z)

    partner = (r + 1 - 2 * core, z)

    def block(index):
        return pl.ds(pl.multiple_of(lax.rem(index + 2 * NZ, NZ) * CH, CH), CH)

    def send(src, dst, s, v, to):
        return pltpu.make_async_remote_copy(
            src_ref=src, dst_ref=dst, send_sem=s, recv_sem=v, device_id=to, device_id_type=MESH
        )

    def each(count, f):
        def body(i, _):
            f(i)
            return 0

        lax.fori_loop(0, count, body, 0)

    def others(f):
        each(NC - 1, lambda i: f(i + 1))

    barrier = pltpu.get_barrier_semaphore()

    def greet(to):
        pl.semaphore_signal(barrier, inc=1, device_id=to, device_id_type=MESH)

    others(lambda d: greet(along(d)))
    others(lambda d: greet(device(chip_at(d))))
    greet(partner)
    pl.semaphore_wait(barrier, 2 * (NC - 1) + 1)

    def rs_copy(way, level, kind):
        sign = 1 - 2 * way
        far = 10 - 2 * level if kind == 0 else 9 - 2 * level
        hop = 2 if kind == 0 else 1
        at = (way * 4 + level - 1) * 2 + kind
        return send(
            part.at[block(z + sign * far)], arrived.at[at],
            rs_send.at[at], rs_recv.at[at], along(sign * hop),
        )

    def rs_list(level):
        return [(w, level, k) for w in (0, 1) for k in (0, 1) if (w, level, k) != (1, 1, 0)]

    def rs_send_level(level):
        for item in rs_list(level):
            rs_copy(*item).start()

    def rs_take_level(level):
        for way in (0, 1):
            sign = 1 - 2 * way
            where = block(z + sign * (8 - 2 * level))
            for item in rs_list(level):
                if item[0] == way:
                    rs_copy(*item).wait_recv()
            for item in rs_list(level):
                if item[0] == way:
                    at = (way * 4 + level - 1) * 2 + item[2]
                    part[where, :] = part[where, :] + arrived[at]

    def ag_copy(way, s, kind):
        sign = 1 - 2 * way
        at = (way * 4 + s - 1) * 2 + kind
        where = block(z - sign * 2 * (s - 1))
        return send(
            full.at[where], full.at[where], ag_send.at[at], ag_recv.at[at],
            along(sign * (2 if kind == 0 else 1)),
        )

    def ag_landing(way, s, kind):
        sign = 1 - 2 * way
        at = (way * 4 + s - 1) * 2 + kind
        where = block(z - sign * (2 * s if kind == 0 else 2 * s - 1))
        return send(
            full.at[where], full.at[where], ag_send.at[at], ag_recv.at[at],
            along(sign * (2 if kind == 0 else 1)),
        )

    def ag_do(s, f):
        for way in (0, 1):
            for kind in (0, 1):
                if (way, kind) == (1, 0):
                    pl.when(s < 4)(lambda way=way, kind=kind: f(way, s, kind))
                else:
                    f(way, s, kind)

    def gz_copy(d):
        return send(piece, gz.at[z], gz_send.at[d], gz_recv.at[z], along(d))

    def gz_landing(d):
        src = lax.rem(z + d, NZ)
        return send(piece, gz.at[src], gz_send.at[d], gz_recv.at[src], along(d))

    def rows_of(index, size):
        return pl.ds(pl.multiple_of(index * size, size), size)

    def scatter_copy(half, into, s, v, size, d):
        to = chip_at(d)
        return send(half.at[rows_of(to, size)], into.at[chip], s.at[d], v.at[chip], device(to))

    def scatter_landing(half, into, s, v, size, d):
        src = chip_at(d)
        return send(half.at[rows_of(src, size)], into.at[src], s.at[d], v.at[src], device(src))

    def gather_copy(own, into, s, v, size, d):
        to = chip_at(d)
        return send(own, into.at[rows_of(core * NC + chip, size)], s.at[d], v.at[chip], device(to))

    def gather_landing(own, into, s, v, size, d):
        src = chip_at(d)
        return send(own, into.at[rows_of(core * NC + src, size)], s.at[d], v.at[src], device(src))

    g_scatter = (g_half, g_in, gs_send, gs_recv, 8)
    p_scatter = (p_half, p_in, ps_send, ps_recv, 16)
    g_gather = (g_own, gram, ga_send, ga_recv, 8)
    v_gather = (g_own, gram_v, va_send, va_recv, 8)
    p_gather = (p_own, back, pa_send, pa_recv, 16)

    def swap_in(array, into, at, size):
        return send(
            array.at[rows_of(1 - core, size)], into, c_send.at[at], c_recv.at[at], partner
        )

    def swap_out(array, at, size):
        half = array.at[rows_of(core, size)]
        return send(half, half, c_send.at[at], c_recv.at[at], partner)

    def swap_landing(array, at, size):
        half = array.at[rows_of(1 - core, size)]
        return send(half, half, c_send.at[at], c_recv.at[at], partner)

    def total(into):
        value = into[0]
        for i in range(1, NC):
            value = value + into[i]
        return value

    first = probe[...]
    xs[:, :R] = first
    xs[:, R:] = jnp.zeros((COLS, 2 * R), BF16)

    def iteration(it, _):
        later = it > 0
        goes_on = it < POWER

        @pl.when(later)
        def _():
            value = feature[...]
            work[:, :R] = dot(value, value, ((0,), (0,)))
            piece[...] = work[rows_of(core * NC + chip, 8), :R]
            gz[z] = piece[...]
            others(lambda d: gz_copy(d).start())
            high, middle, low = split(value)
            xs[:, :R] = high
            xs[:, R : 2 * R] = middle
            xs[:, 2 * R :] = low

        def sketch_rows(i):
            rows = rows_of(i, 256)
            piece_of = delta[rows, :]
            small = dot16(piece_of, xs[:, 2 * R :]) + dot16(piece_of, xs[:, R : 2 * R])
            part[rows, :] = dot16(piece_of, xs[:, :R]) + small

        each(ROWS // 256, sketch_rows)

        rs_send_level(1)
        rs_take_level(1)
        rs_send_level(2)
        rs_take_level(2)
        rs_send_level(3)

        @pl.when(later)
        def _():
            others(lambda d: gz_landing(d).wait_recv())
            mine = total(gz)
            g_own[...] = mine
            gram_v[rows_of(core * NC + chip, 8), :] = mine
            others(lambda d: gather_copy(*v_gather, d).start())

        rs_take_level(3)
        rs_send_level(4)
        rs_take_level(4)
        full[block(z), :] = part[block(z), :]
        ag_do(1, lambda *a: ag_copy(*a).start())

        @pl.when(later)
        def _():
            others(lambda d: gather_landing(*v_gather, d).wait_recv())
            swap_out(gram_v, 2, 128).start()
            swap_landing(gram_v, 2, 128).wait_recv()
            swap_out(gram_v, 2, 128).wait_send()
            others(lambda d: gather_copy(*v_gather, d).wait_send())
            others(lambda d: gz_copy(d).wait_send())
            factor_start(work, gram_v)

        def panel(k):
            pl.when(later)(lambda: factor_panel(work, k))
            ag_do(k + 1, lambda *a: ag_landing(*a).wait_recv())

            @pl.when(k < 3)
            def _():
                ag_do(k + 2, lambda *a: ag_copy(*a).start())

        each(4, panel)
        for level in range(1, 5):
            for item in rs_list(level):
                rs_copy(*item).wait_send()
            ag_do(level, lambda *a: ag_copy(*a).wait_send())

        @pl.when(later)
        def _():
            inv[...] = lower_inverse(work)

            def normal_rows(i):
                rows = rows_of(i, 256)
                basis[rows, :] = dot(full[rows, :], inv[...], ((1,), (1,)))

            each(ROWS // 256, normal_rows)

        @pl.when(jnp.logical_not(later))
        def _():
            basis[...] = full[...]

        value = basis[...]
        gram_part[...] = dot(value, value, ((0,), (0,)))
        swap_in(gram_part, g_half, 0, 128).start()

        @pl.when(goes_on)
        def _():
            high, middle, low = split(basis[...])
            for i in range(2):
                rows = slice(256 * i, 256 * i + 256)
                piece_of = delta_t[rows, :]
                back_part[rows, :] = dot16(piece_of, high) + (
                    dot16(piece_of, middle) + dot16(piece_of, low)
                )
            swap_in(back_part, p_half, 1, 256).start()

        swap_in(gram_part, g_half, 0, 128).wait()
        g_half[...] = g_half[...] + gram_part[rows_of(core, 128), :]
        g_in[chip] = g_half[rows_of(chip, 8), :]
        others(lambda d: scatter_copy(*g_scatter, d).start())

        @pl.when(goes_on)
        def _():
            swap_in(back_part, p_half, 1, 256).wait()
            p_half[...] = p_half[...] + back_part[rows_of(core, 256), :]
            p_in[chip] = p_half[rows_of(chip, 16), :]
            others(lambda d: scatter_copy(*p_scatter, d).start())

        others(lambda d: scatter_landing(*g_scatter, d).wait_recv())
        mine = total(g_in)
        g_own[...] = mine
        gram[rows_of(core * NC + chip, 8), :] = mine
        others(lambda d: gather_copy(*g_gather, d).start())

        @pl.when(goes_on)
        def _():
            others(lambda d: scatter_landing(*p_scatter, d).wait_recv())
            mine = total(p_in)
            p_own[...] = mine
            back[rows_of(core * NC + chip, 16), :] = mine
            others(lambda d: gather_copy(*p_gather, d).start())

        others(lambda d: gather_landing(*g_gather, d).wait_recv())
        swap_out(gram, 3, 128).start()
        swap_landing(gram, 3, 128).wait_recv()
        swap_out(gram, 3, 128).wait_send()
        others(lambda d: scatter_copy(*g_scatter, d).wait_send())
        others(lambda d: gather_copy(*g_gather, d).wait_send())
        factor_start(work, gram)

        @pl.when(goes_on)
        def _():
            others(lambda d: gather_landing(*p_gather, d).wait_recv())
            swap_out(back, 4, 256).start()
            others(lambda d: scatter_copy(*p_scatter, d).wait_send())
            others(lambda d: gather_copy(*p_gather, d).wait_send())

        each(4, lambda k: factor_panel(work, k))

        @pl.when(goes_on)
        def _():
            swap_landing(back, 4, 256).wait_recv()
            swap_out(back, 4, 256).wait_send()
            feature[...] = dot(back[...], lower_inverse(work), ((1,), (1,)))

        return 0

    lax.fori_loop(0, POWER + 1, iteration, 0)

    w_out[...] = math.sqrt(D) * dot(feature[...], inv[...], ((1,), (1,)))
    last = lower_inverse(work)
    at = lax.broadcasted_iota(jnp.int32, (R, R), 0)
    to = lax.broadcasted_iota(jnp.int32, (R, R), 1)
    core_out[...] = jnp.where(at <= to, work[:, :R], 0.0)
    height = q_out.shape[0]
    for start in range(0, height, 256):
        stop = min(start + 256, height)
        rows = dot(basis[start : start + 256, :], last, ((1,), (1,)))
        q_out[start:stop, :] = math.sqrt(FF) * rows[: stop - start, :]


def local(delta, probe):
    row_count = delta.shape[0]
    padded = jnp.pad(delta, ((0, ROWS - row_count), (0, 0)))
    vmem = pl.BlockSpec(memory_space=pltpu.VMEM)

    def floats(*shape):
        return pltpu.VMEM(shape, F32)

    def sems(count):
        return pltpu.SemaphoreType.DMA((count,))

    return pl.pallas_call(
        kernel,
        out_shape=(
            jax.ShapeDtypeStruct((row_count, R), F32),
            jax.ShapeDtypeStruct((COLS, R), F32),
            jax.ShapeDtypeStruct((R, R), F32),
        ),
        in_specs=[vmem] * 3,
        out_specs=(vmem,) * 3,
        scratch_shapes=[
            floats(ROWS, R),
            floats(ROWS, R),
            floats(16, CH, R),
            floats(ROWS, R),
            floats(COLS, R),
            floats(COLS, R),
            floats(COLS, R),
            floats(R, R),
            floats(R, R),
            floats(R, R),
            floats(R, 2 * R),
            floats(R, R),
            pltpu.VMEM((COLS, 3 * R), BF16),
            floats(NZ, 8, R),
            floats(8, R),
            floats(128, R),
            floats(NC, 8, R),
            floats(8, R),
            floats(256, R),
            floats(NC, 16, R),
            floats(16, R),
        ]
        + [sems(16)] * 6
        + [sems(5)] * 2
        + [sems(16)] * 10,
        compiler_params=pltpu.CompilerParams(
            collective_id=0, has_side_effects=True, vmem_limit_bytes=48 << 20
        ),
        cost_estimate=pl.CostEstimate(flops=10**10, bytes_accessed=10**7, transcendentals=0),
        name="range_finder",
    )(padded, padded.T, probe)


def solution(mesh):
    in_specs = (P("row", "col"), P("col", None))
    out_specs = (P("row", None), P("col", None), P())
    return jax.shard_map(local, mesh=mesh, in_specs=in_specs, out_specs=out_specs, check_vma=False)
```

time: 2490 us -> 268 us (0.11)
  waiting for transfers between devices: 1940 us -> 0 us
  other arithmetic: 273 us -> 0 us
  Pallas kernels: 0 us -> 261 us
  blocking collectives: 175 us -> 0 us
  local copies, waits for them, and re-layouts: 32.3 us -> 5.48 us
    psum x7 -> x0, waiting for transfers between devices: 1930 us -> none  [the longest x3 1410 us: range_step(): gram = lax.psum(local_gram(share), ('row', 'col'))]
    another operation x44 -> x0, other arithmetic: 271 us -> none  [the longest x34 173 us: factor(): lower = jnp.linalg.cholesky(gram)]
    pallas_call x0 -> x1, Pallas kernels: none -> 261 us  [local(): pl.pallas_call(kernel, out_shape=(jax.ShapeDtypeStruct((row_count, R), F3...]
    unnamed x3 -> x0, blocking collectives: 95.4 us -> none
    all_gather x3 -> x0, blocking collectives: 79.1 us -> none  [the longest x2 49.9 us: range_step(): full = lax.all_gather(piece.astype(jnp.bfloat16), 'col', axis=0, tiled=True)]
  transfers between devices with their start and end apart: 13 -> 0, of which waited for: 9 -> 0; matrix products, arithmetic and copies ran while one was open for 0% -> 0% of each run, Pallas kernels for 0% -> 0%
where the time goes in v1:
time: 268 us
  Pallas kernels  261 us (97%)
  local copies, waits for them, and re-layouts  5.48 us (2%)
    pallas_call x1, Pallas kernels, local(): pl.pallas_call(kernel, out_shape=(jax.ShapeDtypeStruct((row_count, R), F3...  261 us

profile of v1, /device:TPU:1, one launch (start us, length us, event | category | flops | bytes accessed | tf_op | source)
XLA Modules:
  0.0 267.6 jit_solution(10822371901047406201)
XLA Ops:
  0.6 1.5 copy.5
  2.1 0.5 copy.7
  2.6 0.1 pad_bitcast_fusion.delta_t
  2.8 0.0 copy-start
  2.8 0.1 pad.4.clone.delta
  2.9 0.9 copy-done
  3.7 261.4 %range_finder.1 = (f32[924,256]{1,0:T(8,128)S(1)}, f32[512,256]{1,0:T(8,128)S(1)}, f32[256,256]{1,0:T(8,128)S(1)}) custom-call(bf16[1024,512]{1,0:T(8,128)(2,1)S(1)} %pad.4.clone.delta, bf16[512,1024]{1,0:T(8,128)(2,1)S(1)} %pad_bitcast_fusion.delta_t, bf16[512,256]{1,0:T(8,128)(2,1)S(1)} %copy-done), custom_call_target="tpu_custom_call" | custom-call | flops 10000000000 | bytes 10000000 | tf_op jit(solution)/shard_map/range_finder/pallas_call | solution.py:443
  265.2 0.9 copy.11
  266.1 0.8 copy.12
  266.9 0.7 copy.13
Async XLA Ops:
  2.8 1.0 copy-start

commit v2 on v1

--- a/solution.py
+++ b/solution.py
@@ -19,10 +19,31 @@
 
 NZ = 16
 NC = 16
-CH = 64
-ROWS = NZ * CH
+ROWS = 928
+WIDE = 1024
+LANES = 128
+CH = 120
 COLS = D // NZ
 PANEL = 64
+PARTS = ((0, 32), (32, 32), (64, 32), (96, 24))
+RS_AT = (8, 6, 4, 2, 0)
+AG_AT = (0, 3, 6, 8)
+TILES = ((0, 256), (256, 512), (512, 768), (768, ROWS))
+
+
+def hops(marks):
+    out = []
+    for way in (0, 1):
+        for level in range(len(marks) - 1):
+            for hop in range(abs(marks[level] - marks[level + 1]), 0, -1):
+                far = min(marks[level], marks[level + 1]) + hop
+                if not (way == 1 and far == 8):
+                    out += [(way, level, hop, part) for part in range(len(PARTS))]
+    return out
+
+
+RS_MESSAGES = hops(RS_AT)
+AG_MESSAGES = hops(AG_AT)
 
 
 def dot(a, b, dims):
@@ -77,37 +98,50 @@
     return jnp.concatenate(t, 0)
 
 
-def factor_start(work, gram):
-    at = lax.broadcasted_iota(jnp.int32, (R, R), 0)
-    to = lax.broadcasted_iota(jnp.int32, (R, R), 1)
-    work[:, :R] = gram[...]
-    work[:, R:] = jnp.where(at == to, 1.0, 0.0).astype(F32)
-
-
-def factor_panel(work, k):
-    lane = lax.broadcasted_iota(jnp.int32, (PANEL, 128), 1)
-    row = lax.broadcasted_iota(jnp.int32, (PANEL, 128), 0)
+def factor_panel(work, upper, k):
+    first = k * PANEL
+    tile = first // LANES * LANES
+    odd = k % 2 == 1
+    lane = lax.broadcasted_iota(jnp.int32, (PANEL, LANES), 1)
+    row = lax.broadcasted_iota(jnp.int32, (PANEL, LANES), 0)
     wide = lax.broadcasted_iota(jnp.int32, (PANEL, R), 1)
-    first = pl.multiple_of(k * PANEL, PANEL)
-    panel = work[pl.ds(first, PANEL), :]
-    block = pltpu.roll(panel[:, :R], R - k * PANEL, 1)[:, :128]
+    panel = work[first : first + PANEL, :]
+    block = panel[:, tile : tile + LANES]
+    if odd:
+        block = pltpu.roll(block, PANEL, 1)
     block = jnp.where(lane < PANEL, block, jnp.where(lane == row + PANEL, 1.0, 0.0))
-    inverse = eliminate(block)[:, PANEL : 2 * PANEL]
-    upper = dot(inverse, panel, ((1,), (0,)))
-    work[pl.ds(first, PANEL), :] = upper
-    below = jnp.where(wide >= (k + 1) * PANEL, upper[:, :R], 0.0)
-    work[...] = work[...] - dot(below, upper, ((0,), (0,)))
+    done = eliminate(block)
+    product = dot(done[:, PANEL:], panel, ((1,), (0,)))
+    upper[first : first + PANEL, :] = jnp.where(wide >= first, product, 0.0)
+    placed = done if odd else pltpu.roll(done, PANEL, 1)
+    inside = lane >= PANEL if odd else lane < PANEL
+    pieces = [product[:, at : at + LANES] for at in range(0, R, LANES)]
+    pieces[tile // LANES] = jnp.where(inside, placed, pieces[tile // LANES])
+    fresh = jnp.concatenate(pieces, 1)
+    if first + PANEL < R:
+        start = (first + PANEL) // LANES * LANES
+        left = product[:, start:]
+        if start < first + PANEL:
+            left = jnp.where(wide[:, start:] >= first + PANEL, left, 0.0)
+        at = lax.broadcasted_iota(jnp.int32, (R - start, R), 1)
+        old = jnp.where((at >= first) & (at < first + PANEL), 0.0, work[start:, :])
+        work[start:, :] = old - dot(left, fresh, ((0,), (0,)))
+    work[first : first + PANEL, :] = fresh
+
+
+def norm(gram):
+    return jnp.sqrt(gram[:1, :1])
 
 
 def lower_inverse(work):
     at = lax.broadcasted_iota(jnp.int32, (R, R), 0)
     to = lax.broadcasted_iota(jnp.int32, (R, R), 1)
-    return jnp.where(at >= to, work[:, R:], 0.0)
+    return jnp.where(at >= to, work[...], 0.0)
 
 
 def kernel(
-    delta, delta_t, probe, q_out, w_out, core_out,
-    part, full, arrived, basis, back, back_part, feature, gram, gram_part, gram_v, work, inv, xs, gz, piece,
+    delta, probe, q_out, w_out, core_out,
+    delta_t, part, full, arrived, basis, back, back_part, feature, gram, gram_part, gram_v, work, upper, inv, l_inv, gz, piece,
     g_half, g_in, g_own, p_half, p_in, p_own,
     rs_send, rs_recv, ag_send, ag_recv, gz_send, gz_recv,
     c_send, c_recv, gs_send, gs_recv, ga_send, ga_recv, ps_send, ps_recv, pa_send, pa_recv,
@@ -129,8 +163,9 @@
 
     partner = (r + 1 - 2 * core, z)
 
-    def block(index):
-        return pl.ds(pl.multiple_of(lax.rem(index + 2 * NZ, NZ) * CH, CH), CH)
+    def block(index, part_at):
+        start, size = PARTS[part_at]
+        return pl.ds(pl.multiple_of(lax.rem(index + 2 * NZ, NZ) * CH + start, 8), size)
 
     def send(src, dst, s, v, to):
         return pltpu.make_async_remote_copy(
@@ -145,7 +180,8 @@
         lax.fori_loop(0, count, body, 0)
 
     def others(f):
-        each(NC - 1, lambda i: f(i + 1))
+        for d in range(1, NC):
+            f(d)
 
     barrier = pltpu.get_barrier_semaphore()
 
@@ -155,62 +191,78 @@
     others(lambda d: greet(along(d)))
     others(lambda d: greet(device(chip_at(d))))
     greet(partner)
+
+    def sketch(terms):
+        for start, stop in TILES:
+            stop = min(stop, delta.shape[0])
+            rows = delta[start:stop, :]
+            value = dot16(rows, terms[-1])
+            for term in terms[-2::-1]:
+                value = value + dot16(rows, term)
+            part[start:stop, :] = value[:, :LANES]
+            part[ROWS + start : ROWS + stop, :] = value[:, LANES:]
+
+    def turn():
+        height = delta.shape[0]
+        for start in range(0, WIDE, LANES):
+            rows = delta[start : min(start + LANES, height), :]
+            if start + LANES > height:
+                rest = jnp.zeros((start + LANES - height, COLS), F32)
+                rows = jnp.concatenate([rows.astype(F32), rest], 0).astype(BF16)
+            delta_t[:, start : start + LANES] = rows.T
+
+    for at in (ROWS - 8, 2 * ROWS - 8):
+        part[at : at + 8, :] = jnp.zeros((8, LANES), F32)
+    part[2 * ROWS :, :] = jnp.zeros((NZ * CH - 2 * ROWS, LANES), F32)
+    basis[ROWS:, :] = jnp.zeros((WIDE - ROWS, R), F32)
+    sketch([probe[...]])
     pl.semaphore_wait(barrier, 2 * (NC - 1) + 1)
 
-    def rs_copy(way, level, kind):
-        sign = 1 - 2 * way
-        far = 10 - 2 * level if kind == 0 else 9 - 2 * level
-        hop = 2 if kind == 0 else 1
-        at = (way * 4 + level - 1) * 2 + kind
+    def sign(way, p):
+        return 1 - 2 * ((way + p) % 2)
+
+    def rs_copy(way, level, hop, p):
+        at = RS_MESSAGES.index((way, level, hop, p))
+        to = sign(way, p)
         return send(
-            part.at[block(z + sign * far)], arrived.at[at],
-            rs_send.at[at], rs_recv.at[at], along(sign * hop),
+            part.at[block(z + to * (RS_AT[level + 1] + hop), p)],
+            arrived.at[at, pl.ds(0, PARTS[p][1])],
+            rs_send.at[at], rs_recv.at[at], along(to * hop),
         )
 
-    def rs_list(level):
-        return [(w, level, k) for w in (0, 1) for k in (0, 1) if (w, level, k) != (1, 1, 0)]
-
-    def rs_send_level(level):
-        for item in rs_list(level):
-            rs_copy(*item).start()
-
-    def rs_take_level(level):
+    def rs_start(level, p):
+        for item in RS_MESSAGES:
+            if item[1] == level and item[3] == p:
+                rs_copy(*item).start()
+
+    def rs_take(level, p):
         for way in (0, 1):
-            sign = 1 - 2 * way
-            where = block(z + sign * (8 - 2 * level))
-            for item in rs_list(level):
-                if item[0] == way:
-                    rs_copy(*item).wait_recv()
-            for item in rs_list(level):
-                if item[0] == way:
-                    at = (way * 4 + level - 1) * 2 + item[2]
-                    part[where, :] = part[where, :] + arrived[at]
-
-    def ag_copy(way, s, kind):
-        sign = 1 - 2 * way
-        at = (way * 4 + s - 1) * 2 + kind
-        where = block(z - sign * 2 * (s - 1))
+            where = block(z + sign(way, p) * RS_AT[level + 1], p)
+            value = part[where, :]
+            items = [m for m in RS_MESSAGES if (m[0], m[1], m[3]) == (way, level, p)]
+            for item in items:
+                rs_copy(*item).wait_recv()
+            for item in items:
+                value = value + arrived[RS_MESSAGES.index(item), : PARTS[p][1], :]
+            part[where, :] = value
+
+    def ag_copy(way, level, hop, p, landing=False):
+        at = AG_MESSAGES.index((way, level, hop, p))
+        to = sign(way, p)
+        where = block(z - to * (AG_AT[level] + (hop if landing else 0)), p)
         return send(
-            full.at[where], full.at[where], ag_send.at[at], ag_recv.at[at],
-            along(sign * (2 if kind == 0 else 1)),
+            full.at[where], full.at[where], ag_send.at[at], ag_recv.at[at], along(to * hop)
         )
 
-    def ag_landing(way, s, kind):
-        sign = 1 - 2 * way
-        at = (way * 4 + s - 1) * 2 + kind
-        where = block(z - sign * (2 * s if kind == 0 else 2 * s - 1))
-        return send(
-            full.at[where], full.at[where], ag_send.at[at], ag_recv.at[at],
-            along(sign * (2 if kind == 0 else 1)),
-        )
-
-    def ag_do(s, f):
-        for way in (0, 1):
-            for kind in (0, 1):
-                if (way, kind) == (1, 0):
-                    pl.when(s < 4)(lambda way=way, kind=kind: f(way, s, kind))
-                else:
-                    f(way, s, kind)
+    def ag_start(level, p):
+        for item in AG_MESSAGES:
+            if item[1] == level and item[3] == p:
+                ag_copy(*item).start()
+
+    def ag_take(level, p):
+        for item in AG_MESSAGES:
+            if item[1] == level and item[3] == p:
+                ag_copy(*item, landing=True).wait_recv()
 
     def gz_copy(d):
         return send(piece, gz.at[z], gz_send.at[d], gz_recv.at[z], along(d))
@@ -263,39 +315,41 @@
             value = value + into[i]
         return value
 
-    first = probe[...]
-    xs[:, :R] = first
-    xs[:, R:] = jnp.zeros((COLS, 2 * R), BF16)
-
     def iteration(it, _):
         later = it > 0
         goes_on = it < POWER
+        count = range(len(PARTS))
+
+        for p in count:
+            rs_start(0, p)
 
         @pl.when(later)
         def _():
-            value = feature[...]
-            work[:, :R] = dot(value, value, ((0,), (0,)))
-            piece[...] = work[rows_of(core * NC + chip, 8), :R]
+            factor_panel(work, upper, 2)
+
+        for p in count:
+            rs_take(0, p)
+            rs_start(1, p)
+
+        @pl.when(later)
+        def _():
+            factor_panel(work, upper, 3)
+            l_inv[...] = lower_inverse(work)
+            value = dot(back[...], l_inv[...], ((1,), (1,)))
+            feature[...] = value
+            gram_part[...] = dot(value, value, ((0,), (0,)))
+            piece[...] = gram_part[rows_of(core * NC + chip, 8), :]
             gz[z] = piece[...]
             others(lambda d: gz_copy(d).start())
-            high, middle, low = split(value)
-            xs[:, :R] = high
-            xs[:, R : 2 * R] = middle
-            xs[:, 2 * R :] = low
-
-        def sketch_rows(i):
-            rows = rows_of(i, 256)
-            piece_of = delta[rows, :]
-            small = dot16(piece_of, xs[:, 2 * R :]) + dot16(piece_of, xs[:, R : 2 * R])
-            part[rows, :] = dot16(piece_of, xs[:, :R]) + small
-
-        each(ROWS // 256, sketch_rows)
-
-        rs_send_level(1)
-        rs_take_level(1)
-        rs_send_level(2)
-        rs_take_level(2)
-        rs_send_level(3)
+
+        @pl.when(jnp.logical_not(later))
+        def _():
+            turn()
+
+        for level in (1, 2):
+            for p in count:
+                rs_take(level, p)
+                rs_start(level + 1, p)
 
         @pl.when(later)
         def _():
@@ -305,51 +359,55 @@
             gram_v[rows_of(core * NC + chip, 8), :] = mine
             others(lambda d: gather_copy(*v_gather, d).start())
 
-        rs_take_level(3)
-        rs_send_level(4)
-        rs_take_level(4)
-        full[block(z), :] = part[block(z), :]
-        ag_do(1, lambda *a: ag_copy(*a).start())
+        for p in count:
+            rs_take(3, p)
+            full[block(z, p), :] = part[block(z, p), :]
+            ag_start(0, p)
+        for p in count:
+            ag_take(0, p)
+            ag_start(1, p)
 
         @pl.when(later)
         def _():
             others(lambda d: gather_landing(*v_gather, d).wait_recv())
             swap_out(gram_v, 2, 128).start()
+            others(lambda d: gather_copy(*v_gather, d).wait_send())
+            others(lambda d: gz_copy(d).wait_send())
             swap_landing(gram_v, 2, 128).wait_recv()
             swap_out(gram_v, 2, 128).wait_send()
-            others(lambda d: gather_copy(*v_gather, d).wait_send())
-            others(lambda d: gz_copy(d).wait_send())
-            factor_start(work, gram_v)
-
-        def panel(k):
-            pl.when(later)(lambda: factor_panel(work, k))
-            ag_do(k + 1, lambda *a: ag_landing(*a).wait_recv())
-
-            @pl.when(k < 3)
-            def _():
-                ag_do(k + 2, lambda *a: ag_copy(*a).start())
-
-        each(4, panel)
-        for level in range(1, 5):
-            for item in rs_list(level):
-                rs_copy(*item).wait_send()
-            ag_do(level, lambda *a: ag_copy(*a).wait_send())
+            work[...] = gram_v[...]
+            factor_panel(work, upper, 0)
+
+        for p in count:
+            ag_take(1, p)
+            ag_start(2, p)
 
         @pl.when(later)
         def _():
+            for k in range(1, R // PANEL):
+                factor_panel(work, upper, k)
             inv[...] = lower_inverse(work)
-
-            def normal_rows(i):
-                rows = rows_of(i, 256)
-                basis[rows, :] = dot(full[rows, :], inv[...], ((1,), (1,)))
-
-            each(ROWS // 256, normal_rows)
+            l_inv[...] = norm(gram) * dot(inv[...], l_inv[...], ((1,), (0,)))
+
+        for p in count:
+            ag_take(2, p)
+
+        def sketch_rows(start, stop):
+            return jnp.concatenate(
+                [full[start:stop, :], full[ROWS + start : ROWS + stop, :]], 1
+            )
+
+        @pl.when(later)
+        def _():
+            for start, stop in TILES:
+                basis[start:stop, :] = dot(sketch_rows(start, stop), l_inv[...], ((1,), (1,)))
 
         @pl.when(jnp.logical_not(later))
         def _():
-            basis[...] = full[...]
-
-        value = basis[...]
+            for start, stop in TILES:
+                basis[start:stop, :] = sketch_rows(start, stop)
+
+        value = basis[:ROWS, :]
         gram_part[...] = dot(value, value, ((0,), (0,)))
         swap_in(gram_part, g_half, 0, 128).start()
 
@@ -376,6 +434,10 @@
             p_in[chip] = p_half[rows_of(chip, 16), :]
             others(lambda d: scatter_copy(*p_scatter, d).start())
 
+        for item in RS_MESSAGES:
+            rs_copy(*item).wait_send()
+        for item in AG_MESSAGES:
+            ag_copy(*item).wait_send()
         others(lambda d: scatter_landing(*g_scatter, d).wait_recv())
         mine = total(g_in)
         g_own[...] = mine
@@ -396,7 +458,8 @@
         swap_out(gram, 3, 128).wait_send()
         others(lambda d: scatter_copy(*g_scatter, d).wait_send())
         others(lambda d: gather_copy(*g_gather, d).wait_send())
-        factor_start(work, gram)
+        work[...] = gram[...]
+        factor_panel(work, upper, 0)
 
         @pl.when(goes_on)
         def _():
@@ -405,23 +468,26 @@
             others(lambda d: scatter_copy(*p_scatter, d).wait_send())
             others(lambda d: gather_copy(*p_gather, d).wait_send())
 
-        each(4, lambda k: factor_panel(work, k))
+        factor_panel(work, upper, 1)
 
         @pl.when(goes_on)
         def _():
             swap_landing(back, 4, 256).wait_recv()
             swap_out(back, 4, 256).wait_send()
-            feature[...] = dot(back[...], lower_inverse(work), ((1,), (1,)))
+            sketch(split(back[...] * (1.0 / norm(gram))))
 
         return 0
 
     lax.fori_loop(0, POWER + 1, iteration, 0)
+
+    for k in range(2, R // PANEL):
+        factor_panel(work, upper, k)
 
     w_out[...] = math.sqrt(D) * dot(feature[...], inv[...], ((1,), (1,)))
     last = lower_inverse(work)
     at = lax.broadcasted_iota(jnp.int32, (R, R), 0)
     to = lax.broadcasted_iota(jnp.int32, (R, R), 1)
-    core_out[...] = jnp.where(at <= to, work[:, :R], 0.0)
+    core_out[...] = jnp.where(at <= to, upper[...], 0.0)
     height = q_out.shape[0]
     for start in range(0, height, 256):
         stop = min(start + 256, height)
@@ -431,7 +497,6 @@
 
 def local(delta, probe):
     row_count = delta.shape[0]
-    padded = jnp.pad(delta, ((0, ROWS - row_count), (0, 0)))
     vmem = pl.BlockSpec(memory_space=pltpu.VMEM)
 
     def floats(*shape):
@@ -447,22 +512,24 @@
             jax.ShapeDtypeStruct((COLS, R), F32),
             jax.ShapeDtypeStruct((R, R), F32),
         ),
-        in_specs=[vmem] * 3,
+        in_specs=[vmem] * 2,
         out_specs=(vmem,) * 3,
         scratch_shapes=[
-            floats(ROWS, R),
-            floats(ROWS, R),
-            floats(16, CH, R),
-            floats(ROWS, R),
+            pltpu.VMEM((COLS, WIDE), BF16),
+            floats(NZ * CH, LANES),
+            floats(NZ * CH, LANES),
+            floats(len(RS_MESSAGES), PARTS[0][1], LANES),
+            floats(WIDE, R),
             floats(COLS, R),
             floats(COLS, R),
             floats(COLS, R),
             floats(R, R),
             floats(R, R),
             floats(R, R),
-            floats(R, 2 * R),
-            floats(R, R),
-            pltpu.VMEM((COLS, 3 * R), BF16),
+            floats(R, R),
+            floats(R, R),
+            floats(R, R),
+            floats(R, R),
             floats(NZ, 8, R),
             floats(8, R),
             floats(128, R),
@@ -472,7 +539,9 @@
             floats(NC, 16, R),
             floats(16, R),
         ]
-        + [sems(16)] * 6
+        + [sems(len(RS_MESSAGES))] * 2
+        + [sems(len(AG_MESSAGES))] * 2
+        + [sems(16)] * 2
         + [sems(5)] * 2
         + [sems(16)] * 10,
         compiler_params=pltpu.CompilerParams(
@@ -480,7 +549,7 @@
         ),
         cost_estimate=pl.CostEstimate(flops=10**10, bytes_accessed=10**7, transcendentals=0),
         name="range_finder",
-    )(padded, padded.T, probe)
+    )(delta, probe)
 
 
 def solution(mesh):

time: 268 us -> 231 us (0.86)
  Pallas kernels: 261 us -> 225 us
    pallas_call x1, Pallas kernels: 261 us -> 225 us  [local(): pl.pallas_call(kernel, out_shape=(jax.ShapeDtypeStruct((row_count, R), F3...]
where the time goes in v2:
time: 231 us
  Pallas kernels  225 us (97%)
  local copies, waits for them, and re-layouts  4.56 us (2%)
    pallas_call x1, Pallas kernels, local(): pl.pallas_call(kernel, out_shape=(jax.ShapeDtypeStruct((row_count, R), F3...  225 us

profile of v2, /device:TPU:1, one launch (start us, length us, event | category | flops | bytes accessed | tf_op | source)
XLA Modules:
  0.0 230.7 jit_solution(11492180520684790441)
XLA Ops:
  0.6 0.0 copy-start
  0.6 1.2 copy-done
  1.8 0.0 copy-start.1
  1.8 0.9 copy-done.1
  2.8 225.5 %range_finder.1 = (f32[924,256]{1,0:T(8,128)S(1)}, f32[512,256]{1,0:T(8,128)S(1)}, f32[256,256]{1,0:T(8,128)S(1)}) custom-call(bf16[924,512]{1,0:T(8,128)(2,1)S(1)} %copy-done, bf16[512,256]{1,0:T(8,128)(2,1)S(1)} %copy-done.1), custom_call_target="tpu_custom_call" | custom-call | flops 10000000000 | bytes 10000000 | tf_op jit(solution)/shard_map/range_finder/pallas_call | solution.py:508
  228.3 0.9 copy.8
  229.2 0.8 copy.9
  230.0 0.7 copy.10
Async XLA Ops:
  0.6 1.2 copy-start
  1.8 0.9 copy-start.1

commit v3 on v2

--- a/solution.py
+++ b/solution.py
@@ -27,8 +27,11 @@
 PANEL = 64
 PARTS = ((0, 32), (32, 32), (64, 32), (96, 24))
 RS_AT = (8, 6, 4, 2, 0)
-AG_AT = (0, 3, 6, 8)
+AG_AT = (0, 2, 5, 8)
 TILES = ((0, 256), (256, 512), (512, 768), (768, ROWS))
+
+PLANE_ORDER = (10, 6, 14, 9, 11, 2, 8, 5, 7, 13, 15, 1, 3, 4, 12)
+LINE_ORDER = (8, 7, 9, 6, 10, 5, 11, 4, 12, 3, 13, 2, 14, 1, 15)
 
 
 def hops(marks):
@@ -56,10 +59,16 @@
 
 def split(x):
     high = x.astype(BF16)
-    rest = x - high.astype(F32)
-    middle = rest.astype(BF16)
-    low = (rest - middle.astype(F32)).astype(BF16)
-    return high, middle, low
+    return high, (x - high.astype(F32)).astype(BF16)
+
+
+def dot_t(a, b):
+    def part(x, y):
+        return lax.dot_general(x, y, (((1,), (1,)), ((), ())), preferred_element_type=F32)
+
+    a_high, a_low = split(a)
+    b_high, b_low = b
+    return part(a_high, b_high) + (part(a_high, b_low) + part(a_low, b_high))
 
 
 def eliminate(block):
@@ -179,8 +188,8 @@
 
         lax.fori_loop(0, count, body, 0)
 
-    def others(f):
-        for d in range(1, NC):
+    def others(f, order=PLANE_ORDER):
+        for d in order:
             f(d)
 
     barrier = pltpu.get_barrier_semaphore()
@@ -335,22 +344,26 @@
         def _():
             factor_panel(work, upper, 3)
             l_inv[...] = lower_inverse(work)
-            value = dot(back[...], l_inv[...], ((1,), (1,)))
+            value = dot_t(back[...], split(l_inv[...]))
             feature[...] = value
             gram_part[...] = dot(value, value, ((0,), (0,)))
             piece[...] = gram_part[rows_of(core * NC + chip, 8), :]
             gz[z] = piece[...]
-            others(lambda d: gz_copy(d).start())
+            others(lambda d: gz_copy(d).start(), LINE_ORDER)
 
         @pl.when(jnp.logical_not(later))
         def _():
             turn()
 
-        for level in (1, 2):
+        for level in range(1, len(RS_AT) - 2):
             for p in count:
                 rs_take(level, p)
                 rs_start(level + 1, p)
 
+        for p in count:
+            rs_take(len(RS_AT) - 2, p)
+            full[block(z, p), :] = part[block(z, p), :]
+            ag_start(0, p)
         @pl.when(later)
         def _():
             others(lambda d: gz_landing(d).wait_recv())
@@ -359,10 +372,6 @@
             gram_v[rows_of(core * NC + chip, 8), :] = mine
             others(lambda d: gather_copy(*v_gather, d).start())
 
-        for p in count:
-            rs_take(3, p)
-            full[block(z, p), :] = part[block(z, p), :]
-            ag_start(0, p)
         for p in count:
             ag_take(0, p)
             ag_start(1, p)
@@ -399,8 +408,9 @@
 
         @pl.when(later)
         def _():
+            terms = split(l_inv[...])
             for start, stop in TILES:
-                basis[start:stop, :] = dot(sketch_rows(start, stop), l_inv[...], ((1,), (1,)))
+                basis[start:stop, :] = dot_t(sketch_rows(start, stop), terms)
 
         @pl.when(jnp.logical_not(later))
         def _():
@@ -413,13 +423,11 @@
 
         @pl.when(goes_on)
         def _():
-            high, middle, low = split(basis[...])
+            high, low = split(basis[...])
             for i in range(2):
                 rows = slice(256 * i, 256 * i + 256)
                 piece_of = delta_t[rows, :]
-                back_part[rows, :] = dot16(piece_of, high) + (
-                    dot16(piece_of, middle) + dot16(piece_of, low)
-                )
+                back_part[rows, :] = dot16(piece_of, high) + dot16(piece_of, low)
             swap_in(back_part, p_half, 1, 256).start()
 
         swap_in(gram_part, g_half, 0, 128).wait()
@@ -433,6 +441,10 @@
             p_half[...] = p_half[...] + back_part[rows_of(core, 256), :]
             p_in[chip] = p_half[rows_of(chip, 16), :]
             others(lambda d: scatter_copy(*p_scatter, d).start())
+
+        @pl.when(jnp.logical_not(goes_on))
+        def _():
+            w_out[...] = math.sqrt(D) * dot_t(feature[...], split(inv[...]))
 
         for item in RS_MESSAGES:
             rs_copy(*item).wait_send()
@@ -483,15 +495,14 @@
     for k in range(2, R // PANEL):
         factor_panel(work, upper, k)
 
-    w_out[...] = math.sqrt(D) * dot(feature[...], inv[...], ((1,), (1,)))
-    last = lower_inverse(work)
+    last = split(lower_inverse(work))
     at = lax.broadcasted_iota(jnp.int32, (R, R), 0)
     to = lax.broadcasted_iota(jnp.int32, (R, R), 1)
     core_out[...] = jnp.where(at <= to, upper[...], 0.0)
     height = q_out.shape[0]
     for start in range(0, height, 256):
         stop = min(start + 256, height)
-        rows = dot(basis[start : start + 256, :], last, ((1,), (1,)))
+        rows = dot_t(basis[start : start + 256, :], last)
         q_out[start:stop, :] = math.sqrt(FF) * rows[: stop - start, :]
 
 

time: 231 us -> 215 us (0.931)
  Pallas kernels: 225 us -> 210 us
    pallas_call x1, Pallas kernels: 225 us -> 210 us  [local(): pl.pallas_call(kernel, out_shape=(jax.ShapeDtypeStruct((row_count, R), F3...]
where the time goes in v3:
time: 215 us
  Pallas kernels  210 us (98%)
  local copies, waits for them, and re-layouts  4.56 us (2%)
    pallas_call x1, Pallas kernels, local(): pl.pallas_call(kernel, out_shape=(jax.ShapeDtypeStruct((row_count, R), F3...  210 us
    unnamed x7, local copies, waits for them, and re-layouts  4.56 us

profile of v3, /device:TPU:1, one launch (start us, length us, event | category | flops | bytes accessed | tf_op | source)
XLA Modules:
  0.0 215.1 jit_solution(1154008211999582689)
XLA Ops:
  0.6 0.0 copy-start
  0.6 1.2 copy-done
  1.8 0.0 copy-start.1
  1.8 0.9 copy-done.1
  2.8 209.9 %range_finder.1 = (f32[924,256]{1,0:T(8,128)S(1)}, f32[512,256]{1,0:T(8,128)S(1)}, f32[256,256]{1,0:T(8,128)S(1)}) custom-call(bf16[924,512]{1,0:T(8,128)(2,1)S(1)} %copy-done, bf16[512,256]{1,0:T(8,128)(2,1)S(1)} %copy-done.1), custom_call_target="tpu_custom_call" | custom-call | flops 10000000000 | bytes 10000000 | tf_op jit(solution)/shard_map/range_finder/pallas_call | solution.py:519
  212.7 0.9 copy.8
  213.6 0.8 copy.9
  214.4 0.7 copy.10
Async XLA Ops:
  0.6 1.2 copy-start
  1.8 0.9 copy-start.1
